TPU v7x, 32 devices: a whole 2x2x4 slice. The times are simulated.
32 devices in a mesh: wide: 8 (over z, y), narrow: 4 (over x, core).
Axes of the slice: x: 2, y: 2, z: 4, core: 2. Of those that a mesh axis runs over, the one named last changes fastest.
Arguments:
- tokens: bfloat16 [4096, 1024], P('wide'), may hold values from -1.5 to 1.5
- w_qk1: bfloat16 [1024, 1024], P(None, 'narrow')
- w_value1: bfloat16 [1024, 1024], P(None, 'narrow'), may hold values from -0.1875 to 0.1875
- w_out1: bfloat16 [1024, 1024], P('narrow'), may hold values from -0.1875 to 0.1875
- w_qk2: bfloat16 [1024, 1024], P(None, 'narrow')
- w_value2: bfloat16 [1024, 1024], P(None, 'narrow'), may hold values from -0.1875 to 0.1875
- w_out2: bfloat16 [1024, 1024], P('narrow'), may hold values from -0.5 to 0.5
- cluster_ids: int32 [8, 4096], P('narrow', 'wide'), may hold values from 0 to 3, as said below
Outputs:
- layer_out: float32 [4096, 1024], P('wide', 'narrow')
Inputs may be any that keep to these rules, and one draw needn't show every extreme that they name: `cluster_ids`: within the 512 tokens of one index of wide, for each head, a quarter of the clusters hold 256 tokens each, half hold 96 and a quarter hold 64; which clusters are which is the same in every such block of one head.
All inputs are finite; a program needn't handle non-finite values.
Results may differ from a plain program's by a relative error of at most 0.022.
Values may be sent and summed in bfloat16 or wider, within the bound.
A program may use at most 64 MiB of HBM per device.

v0:
```python
import functools
import math

import jax
import jax.numpy as jnp
from jax import lax
from jax.experimental import pallas as pl
from jax.experimental.pallas import tpu as pltpu
from jax.sharding import PartitionSpec as P

HEAD_DIM = 128
WINDOW = 256
EPS = 1e-06
BLOCK = 256
SCALE = math.log2(math.e) / math.sqrt(HEAD_DIM)
LOW = -1e30
MESH = pl.DeviceIdType.MESH
F32 = jnp.float32
BF16 = jnp.bfloat16


def flip(index, bit):
    return index + bit - 2 * bit * lax.rem(lax.div(index, bit), 2)


def rms_round(rows):
    values = rows.astype(F32)
    factor = lax.rsqrt(jnp.mean(values * values, axis=-1, keepdims=True) + EPS)
    return (values * factor).astype(BF16)


def dot(a, b):
    return jnp.dot(a, b, preferred_element_type=F32)


def dot_nt(a, b):
    return lax.dot_general(a, b, (((1,), (1,)), ((), ())), preferred_element_type=F32)


def dot_tn(a, b):
    return lax.dot_general(a, b, (((0,), (0,)), ((), ())), preferred_element_type=F32)


def send(src, dst, send_sem, recv_sem, **where):
    return pltpu.make_async_remote_copy(
        src_ref=src, dst_ref=dst, send_sem=send_sem, recv_sem=recv_sem,
        device_id=where, device_id_type=MESH)


def whole_kernel(wide_n, heads, clusters, sizes, pads, slots,
                 tokens, w_qk1, w_value1, w_out1, w_qk2, w_value2, w_out2, ids, out,
                 kvx, w1, att1, hidden, normed2, to_slot, to_token, packed, arrived, value_t, answers, ret, att2, w2,
                 halo_sem, w1_sems, att1_sems, w2_sems, go_s, go_r, back_s, back_r, att2_sems, local_sem):
    me, n = lax.axis_index("wide"), lax.axis_index("narrow")
    near, far = flip(n, 1), flip(n, 2)
    cross = flip(near, 2)
    length = tokens.shape[0]
    cols = w_qk1.shape[1]
    counts = (clusters // 4, clusters // 2, clusters // 4)
    starts = (0, clusters // 4, 3 * clusters // 4)
    bases = (0, counts[0] * pads[0], counts[0] * pads[0] + counts[1] * pads[1])
    core = lax.rem(n, 2)

    def shuffle(place):
        low = flip(place, 2)
        high = flip(place, 1)
        return jnp.where(place < wide_n // 2, low, high)

    def flip_core(place):
        return jnp.where(core == 1, flip(place, 1), place)

    def device_of(owner):
        return flip_core(shuffle(owner))

    mine = shuffle(flip_core(me))
    my_head, my_rank = lax.div(mine, clusters), lax.rem(mine, clusters)

    barrier = pltpu.get_barrier_semaphore()

    @pl.loop(1, wide_n)
    def _(k):
        pl.semaphore_signal(barrier, inc=1, device_id={"wide": lax.rem(me + k, wide_n)}, device_id_type=MESH)

    for other in (near, far, cross):
        pl.semaphore_signal(barrier, inc=1, device_id={"narrow": other}, device_id_type=MESH)

    def project1(start):
        rows = pl.ds(start, BLOCK)
        normed = rms_round(tokens[rows, :])
        there = pl.ds(WINDOW + start, BLOCK)
        kvx[there, pl.ds(0, cols)] = dot(normed, w_qk1[...]).astype(BF16)
        kvx[there, pl.ds(cols, cols)] = dot(normed, w_value1[...]).astype(BF16)

    tail = length - BLOCK
    half_rows = cols // 2
    beside = flip(me, 2)
    parity = lax.rem(lax.div(me, 2), 2)
    early = pl.ds(pl.multiple_of(parity * half_rows, half_rows), half_rows)
    late = pl.ds(pl.multiple_of((1 - parity) * half_rows, half_rows), half_rows)
    w1_far = send(w_out1.at[early], w1.at[n, early], w1_sems.at[0, 0], w1_sems.at[1, 0], narrow=far)
    w1_near = send(w_out1, w1.at[n], w1_sems.at[0, 1], w1_sems.at[1, 1], narrow=near)
    w1_swap = send(w1.at[far, early], w1.at[far, early], w1_sems.at[0, 2], w1_sems.at[1, 2], wide=beside)
    w1_fwd = (send(w1.at[far, early], w1.at[far, early], w1_sems.at[0, 3], w1_sems.at[1, 3], narrow=near),
              send(w1.at[far, late], w1.at[far, late], w1_sems.at[0, 4], w1_sems.at[1, 4], narrow=near))
    halo = send(kvx.at[pl.ds(length, WINDOW)], kvx.at[pl.ds(0, WINDOW)], halo_sem.at[0], halo_sem.at[1],
                wide=lax.rem(me + 1, wide_n))
    project1(tail)
    pl.semaphore_wait(barrier, wide_n - 1 + 3)
    w1_far.start()

    @pl.when(me < wide_n - 1)
    def _():
        halo.start()

    w1_near.start()

    @pl.when(me == 0)
    def _():
        kvx[pl.ds(0, WINDOW), :] = jnp.zeros((WINDOW, 2 * cols), BF16)

    project1(0)

    def window(start):
        key_at = lax.broadcasted_iota(jnp.int32, (2 * BLOCK, BLOCK), 0) + (me * length + start - WINDOW)
        query_at = lax.broadcasted_iota(jnp.int32, (2 * BLOCK, BLOCK), 1) + (me * length + start)
        gap = query_at - key_at
        keep = (gap > 0) & (gap < WINDOW) & (key_at >= 0) | (gap == 0) & (query_at == 0)
        for h in range(heads):
            q = kvx[pl.ds(start + WINDOW, BLOCK), pl.ds(h * HEAD_DIM, HEAD_DIM)]
            k = kvx[pl.ds(start, 2 * BLOCK), pl.ds(h * HEAD_DIM, HEAD_DIM)]
            v = kvx[pl.ds(start, 2 * BLOCK), pl.ds(cols + h * HEAD_DIM, HEAD_DIM)]
            scores = jnp.where(keep, dot_nt(k, q) * SCALE, LOW)
            top = jnp.max(scores, axis=0, keepdims=True)
            weights = jnp.exp2(scores - top)
            total = jnp.sum(weights, axis=0, keepdims=True)
            mixed = dot_tn(v, weights.astype(BF16)) / total
            att1[n, pl.ds(start, BLOCK), pl.ds(h * HEAD_DIM, HEAD_DIM)] = mixed.T.astype(BF16)

    def share(buffer, sems, half):
        rows = pl.ds(half * BLOCK, BLOCK)
        first = send(buffer.at[n, rows], buffer.at[n, rows], sems.at[0, half, 0], sems.at[1, half, 0], narrow=far)
        second = send(buffer.at[n, rows], buffer.at[n, rows], sems.at[0, half, 1], sems.at[1, half, 1], narrow=near)
        third = send(buffer.at[far, rows], buffer.at[far, rows], sems.at[0, half, 2], sems.at[1, half, 2],
                     narrow=near)
        return first, second, third

    att1_sends = [share(att1, att1_sems, half) for half in range(2)]
    window(tail)
    att1_sends[1][0].start()
    att1_sends[1][1].start()
    w1_far.wait_recv()
    w1_swap.start()
    w1_fwd[0].start()

    @pl.when(me > 0)
    def _():
        halo.wait_recv()

    window(0)
    att1_sends[0][0].start()
    att1_sends[0][1].start()

    w1[n] = w_out1[...]

    most = 128
    before = (lax.broadcasted_iota(jnp.int32, (length, length), 0)
              <= lax.broadcasted_iota(jnp.int32, (length, length), 1)).astype(F32).astype(BF16)
    for h in range(heads):
        match = (lax.broadcasted_iota(jnp.int32, (most, length), 0) == ids[pl.ds(h, 1), :]).astype(F32)
        match16 = match.astype(BF16)
        running = dot(match16, before)
        held = jnp.sum(match, axis=1, keepdims=True)
        held_row = dot_nt(jnp.ones((8, length), BF16), match16)[0:1, :]
        lower = (lax.broadcasted_iota(jnp.int32, (most, most), 1)
                 < lax.broadcasted_iota(jnp.int32, (most, most), 0))
        ahead = (held_row > held) | (held_row == held) & lower
        rank = jnp.sum(ahead.astype(F32), axis=1, keepdims=True)
        base = jnp.where(
            rank < starts[1], rank * pads[0],
            jnp.where(rank < starts[2], bases[1] + (rank - starts[1]) * pads[1],
                      bases[2] + (rank - starts[2]) * pads[2]))
        target = jnp.sum(match * (base + running - 1.0), axis=0, keepdims=True)
        target_col = jnp.broadcast_to(target, (8, length)).T[:, 0:1].astype(jnp.int32)
        target = target.astype(jnp.int32)
        to_slot[h] = (lax.broadcasted_iota(jnp.int32, (slots, length), 0) == target).astype(F32).astype(BF16)
        to_token[h] = (lax.broadcasted_iota(jnp.int32, (length, slots), 1) == target_col).astype(F32).astype(BF16)

    att1_sends[1][0].wait_recv()
    att1_sends[1][2].start()
    w1_swap.wait_recv()
    w1_fwd[1].start()
    att1_sends[0][0].wait_recv()
    att1_sends[0][2].start()
    w1_near.wait_recv()
    w1_fwd[0].wait_recv()
    w1_fwd[1].wait_recv()

    for half in (1, 0):
        first, second, third = att1_sends[half]
        second.wait_recv()
        third.wait_recv()
        rows = pl.ds(half * BLOCK, BLOCK)
        total = tokens[rows, :].astype(F32)
        for g in range(4):
            total = total + dot(att1[g, rows, :], w1[g])
        hidden16 = total.astype(BF16)
        hidden[rows, :] = hidden16
        normed2[rows, :] = rms_round(hidden16)

    def place(level, head, step):
        rank = starts[level] + step
        owner = head * clusters + rank
        offset = pl.multiple_of(bases[level] + step * pads[level], 16)
        return owner, device_of(owner), offset

    def go(level, head, step):
        owner, there, offset = place(level, head, step)
        size = pads[level]
        return there, send(packed.at[head, pl.ds(offset, size)],
                           arrived.at[pl.ds(pl.multiple_of(me * size, 16), size)],
                           go_s.at[owner], go_r.at[me], wide=there), (head, offset, size)

    def each_owner(body):
        for level in range(3):
            @pl.loop(0, heads * counts[level])
            def _(item):
                body(level, lax.div(item, counts[level]), lax.rem(item, counts[level]))

    def start_go(level, head, step):
        there, copy, (_, offset, size) = go(level, head, step)

        @pl.when(there != me)
        def _():
            copy.start()

        @pl.when(there == me)
        def _():
            own = pltpu.make_async_copy(packed.at[head, pl.ds(offset, size)],
                                        arrived.at[pl.ds(pl.multiple_of(me * size, 16), size)], local_sem)
            own.start()
            own.wait()

    for h in range(heads):
        part = pl.ds(h * HEAD_DIM, HEAD_DIM)
        both = jnp.concatenate([w_qk2[:, part], w_value2[:, part]], axis=1)
        packed[h] = dot(to_slot[h], dot(normed2[...], both).astype(BF16)).astype(BF16)
        for level in range(3):
            @pl.loop(0, counts[level])
            def _(step):
                start_go(level, h, step)

    w2_sends = []
    for index, other in enumerate((near, far, cross)):
        w2_sends.append(send(w_out2.at[:, pl.ds(pl.multiple_of(other * cols, cols), cols)], w2.at[n],
                             w2_sems.at[0, index], w2_sems.at[1, index], narrow=other))
        w2_sends[-1].start()
    w2[n] = w_out2[:, pl.ds(pl.multiple_of(n * cols, cols), cols)]

    def for_level(body):
        for level in range(3):
            @pl.when((my_rank >= starts[level]) & (my_rank < starts[level] + counts[level]))
            def _():
                body(level)

    def from_source(level, source):
        size = pads[level]
        rows = pl.ds(pl.multiple_of(source * size, 16), size)
        return send(packed.at[0, pl.ds(0, size)], arrived.at[rows], go_s.at[0], go_r.at[source], wide=source)

    def back_copy(level, source):
        size = pads[level]
        rows = pl.ds(pl.multiple_of(source * size, 16), size)
        offset = pl.multiple_of(bases[level] + (my_rank - starts[level]) * size, 16)
        return rows, offset, send(answers.at[rows], ret.at[my_head, pl.ds(offset, size)],
                                  back_s.at[source], back_r.at[mine], wide=source)

    def receive(level, source):
        @pl.when(source != me)
        def _():
            from_source(level, source).wait_recv()

    def give_back(level, source):
        rows, offset, copy = back_copy(level, source)

        @pl.when(source != me)
        def _():
            copy.start()

        @pl.when(source == me)
        def _():
            own = pltpu.make_async_copy(answers.at[rows], ret.at[my_head, pl.ds(offset, pads[level])], local_sem)
            own.start()
            own.wait()

    def attend(level, block):
        size, real = pads[level], sizes[level]
        begin = block * BLOCK
        here = pl.ds(begin, BLOCK)
        q = arrived[here, pl.ds(0, HEAD_DIM)]
        value_t[:, here] = arrived[here, pl.ds(HEAD_DIM, HEAD_DIM)].T

        def score(first, rows, diagonal):
            scores = dot_nt(arrived[pl.ds(first, rows), pl.ds(0, HEAD_DIM)], q) * SCALE
            keep = None
            key_at = lax.broadcasted_iota(jnp.int32, (rows, BLOCK), 0)
            if diagonal:
                query_at = lax.broadcasted_iota(jnp.int32, (rows, BLOCK), 1)
                keep = key_at < query_at
                if block == 0:
                    keep = keep | (key_at + query_at == 0)
            if size != real:
                live = lax.rem(key_at + first, size) < real
                keep = live if keep is None else keep & live
            return scores if keep is None else jnp.where(keep, scores, LOW)

        parts = [(begin, score(begin, BLOCK, True))]
        if block > 0:
            parts.append((0, score(0, begin, False)))
        top = functools.reduce(jnp.maximum, [jnp.max(scores, axis=0, keepdims=True) for _, scores in parts])
        total, mixed = 0.0, 0.0
        for first, scores in parts:
            weights = jnp.exp2(scores - top)
            total = total + jnp.sum(weights, axis=0, keepdims=True)
            mixed = mixed + dot(value_t[:, pl.ds(first, scores.shape[0])], weights.astype(BF16))
        answers[here, :] = (mixed / total).T.astype(BF16)

    def own_clusters(level):
        blocks = wide_n * pads[level] // BLOCK
        if pads[level] == BLOCK:
            for block in range(blocks):
                receive(level, block)
                attend(level, block)
                give_back(level, block)
        else:
            @pl.loop(0, wide_n)
            def _(source):
                receive(level, source)

            for block in range(blocks):
                attend(level, block)

            @pl.loop(0, wide_n)
            def _(source):
                give_back(level, source)

    for_level(own_clusters)

    def wait_back(level, head, step):
        owner, there, offset = place(level, head, step)
        size = pads[level]

        @pl.when(there != me)
        def _():
            send(answers.at[pl.ds(0, size)], ret.at[head, pl.ds(offset, size)],
                 back_s.at[0], back_r.at[owner], wide=there).wait_recv()

    each_owner(wait_back)
    att2_sends = [share(att2, att2_sems, half) for half in range(2)]
    for half in range(2):
        rows = pl.ds(half * BLOCK, BLOCK)
        for h in range(heads):
            att2[n, rows, pl.ds(h * HEAD_DIM, HEAD_DIM)] = dot(to_token[h, rows, :], ret[h]).astype(BF16)
        att2_sends[half][0].start()
        att2_sends[half][1].start()
    for copy in w2_sends:
        copy.wait_recv()
    for half in range(2):
        att2_sends[half][0].wait_recv()
        att2_sends[half][2].start()
    for half in range(2):
        rows = pl.ds(half * BLOCK, BLOCK)
        att2_sends[half][1].wait_recv()
        att2_sends[half][2].wait_recv()
        total = hidden[rows, pl.ds(pl.multiple_of(n * cols, cols), cols)].astype(F32)
        for g in range(4):
            total = total + dot(att2[g, rows, :], w2[g])
        out[rows, :] = total

    for copy in (w1_far, w1_near, w1_swap, *w1_fwd, *w2_sends, *att1_sends[0], *att1_sends[1], *att2_sends[0], *att2_sends[1]):
        copy.wait_send()

    @pl.when(me < wide_n - 1)
    def _():
        halo.wait_send()

    def sent(level, head, step):
        there, copy, _ = go(level, head, step)

        @pl.when(there != me)
        def _():
            copy.wait_send()

    each_owner(sent)

    def sent_back(level):
        @pl.loop(0, wide_n)
        def _(source):
            @pl.when(source != me)
            def _():
                back_copy(level, source)[2].wait_send()

    for_level(sent_back)


def solution(mesh):
    wide_n = mesh.shape["wide"]

    def shards(tokens, w_qk1, w_value1, w_out1, w_qk2, w_value2, w_out2, cluster_ids):
        length, width = tokens.shape
        cols = w_qk1.shape[1]
        heads = cols // HEAD_DIM
        clusters = wide_n // heads
        cap = 2 * length * heads // wide_n
        sizes = (cap, 3 * cap // 8, cap // 4)
        pads = tuple(-(-size // 16) * 16 for size in sizes)
        slots = clusters // 4 * pads[0] + clusters // 2 * pads[1] + clusters // 4 * pads[2]
        most = wide_n * pads[0]
        groups = mesh.shape["narrow"]
        dma = pltpu.SemaphoreType.DMA
        vmem = pl.BlockSpec(memory_space=pltpu.VMEM)
        return pl.pallas_call(
            functools.partial(whole_kernel, wide_n, heads, clusters, sizes, pads, slots),
            out_shape=jax.ShapeDtypeStruct((length, cols), F32),
            in_specs=[vmem] * 8,
            out_specs=vmem,
            scratch_shapes=[
                pltpu.VMEM((WINDOW + length, 2 * cols), BF16),
                pltpu.VMEM((groups, cols, width), BF16),
                pltpu.VMEM((groups, length, cols), BF16),
                pltpu.VMEM((length, width), BF16),
                pltpu.VMEM((length, width), BF16),
                pltpu.VMEM((heads, slots, length), BF16),
                pltpu.VMEM((heads, length, slots), BF16),
                pltpu.VMEM((heads, slots, 2 * HEAD_DIM), BF16),
                pltpu.VMEM((most, 2 * HEAD_DIM), BF16),
                pltpu.VMEM((HEAD_DIM, most), BF16),
                pltpu.VMEM((most, HEAD_DIM), BF16),
                pltpu.VMEM((heads, slots, HEAD_DIM), BF16),
                pltpu.VMEM((groups, length, cols), BF16),
                pltpu.VMEM((groups, cols, cols), BF16),
                dma((2,)), dma((2, 5)), dma((2, 2, 3)), dma((2, 3)),
                dma((wide_n,)), dma((wide_n,)), dma((wide_n,)), dma((wide_n,)),
                dma((2, 2, 3)), dma,
            ],
            compiler_params=pltpu.CompilerParams(
                collective_id=0, has_side_effects=True, vmem_limit_bytes=56 * 1024 * 1024),
        )(tokens, w_qk1, w_value1, w_out1, w_qk2, w_value2, w_out2, cluster_ids)

    placed = (
        P("wide", None),
        P(None, "narrow"),
        P(None, "narrow"),
        P("narrow", None),
        P(None, "narrow"),
        P(None, "narrow"),
        P("narrow", None),
        P("narrow", "wide"),
    )
    return jax.shard_map(
        shards, mesh=mesh, in_specs=placed, out_specs=P("wide", "narrow"), check_vma=False
    )
```

profile of v0, /device:TPU:0, one launch (start us, length us, event | category | flops | bytes accessed | tf_op | source)
XLA Modules:
  0.0 57.6 jit_solution(4115769441128164029)
XLA Ops:
  0.0 55.7 %shard_map.82 = f32[512,256]{1,0:T(8,128)} custom-call(bf16[512,1024]{1,0:T(8,128)(2,1)} %tokens.1, bf16[1024,256]{1,0:T(8,128)(2,1)} %w_qk1.1, bf16[1024,256]{1,0:T(8,128)(2,1)} %w_value1.1, bf16[256,1024]{1,0:T(8,128)(2,1)} %w_out1.1, bf16[1024,256]{1,0:T(8,128)(2,1)} %w_qk2.1, bf16[1024,256]{1,0:T(8,128)(2,1)} %w_value2.1, bf16[256,1024]{1,0:T(8,128)(2,1)} %w_out2.1, ...), custom_call_target="tpu_custom_call" | custom-call | tf_op jit(solution)/shard_map/pallas_call | solution.py:421
  55.7 1.9 %copy.10 = f32[512,256]{1,0:T(8,128)} copy(f32[512,256]{1,0:T(8,128)} %shard_map.82) | data formatting | bytes 1048576
where the time goes:
time: 57.8 us; the launch traced here: 57.6 us
  Pallas kernels  55.7 us (96%)
  local copies, waits for them, and re-layouts  1.87 us (3%)
    pallas_call x1, Pallas kernels, shards(): pl.pallas_call(functools.partial(whole_kernel, wide_n, heads, clusters, s...  55.7 us
    unnamed x1, local copies, waits for them, and re-layouts  1.87 us

commit v1 on v0

--- a/solution.py
+++ b/solution.py
@@ -48,13 +48,13 @@
 
 
 def whole_kernel(wide_n, heads, clusters, sizes, pads, slots,
-                 tokens, w_qk1, w_value1, w_out1, w_qk2, w_value2, w_out2, ids, out,
-                 kvx, w1, att1, hidden, normed2, to_slot, to_token, packed, arrived, value_t, answers, ret, att2, w2,
-                 halo_sem, w1_sems, att1_sems, w2_sems, go_s, go_r, back_s, back_r, att2_sems, local_sem):
+                 tokens_in, w_qk1, w_value1, w_out1, w_qk2, w_value2, w_out2, ids_in, out,
+                 tokens, wkv1, wkv2, ids, kvx, w1, att1, hidden, normed2, to_slot, to_token, packed, arrived, value_t, answers, ret, att2, w2,
+                 halo_sem, w1_sems, att1_sems, w2_sems, go_s, go_r, back_s, back_r, att2_sems, local_sem, load_sems):
     me, n = lax.axis_index("wide"), lax.axis_index("narrow")
     near, far = flip(n, 1), flip(n, 2)
     cross = flip(near, 2)
-    length = tokens.shape[0]
+    length = tokens_in.shape[0]
     cols = w_qk1.shape[1]
     counts = (clusters // 4, clusters // 2, clusters // 4)
     starts = (0, clusters // 4, 3 * clusters // 4)
@@ -84,29 +84,44 @@
     for other in (near, far, cross):
         pl.semaphore_signal(barrier, inc=1, device_id={"narrow": other}, device_id_type=MESH)
 
+    mine_cols = pl.ds(pl.multiple_of(n * cols, cols), cols)
+    loads = [(tokens_in, tokens), (w_qk1, wkv1.at[:, pl.ds(0, cols)]), (w_value1, wkv1.at[:, pl.ds(cols, cols)]),
+             (ids_in, ids), (w_out1, w1.at[n]), (w_out2.at[:, mine_cols], w2.at[n])]
+    for h in range(heads):
+        part = pl.ds(h * HEAD_DIM, HEAD_DIM)
+        loads.append((w_qk2.at[:, part], wkv2.at[h, :, pl.ds(0, HEAD_DIM)]))
+        loads.append((w_value2.at[:, part], wkv2.at[h, :, pl.ds(HEAD_DIM, HEAD_DIM)]))
+    loads = [pltpu.make_async_copy(src, dst, load_sems.at[index]) for index, (src, dst) in enumerate(loads)]
+    for copy in loads:
+        copy.start()
+
     def project1(start):
         rows = pl.ds(start, BLOCK)
         normed = rms_round(tokens[rows, :])
         there = pl.ds(WINDOW + start, BLOCK)
-        kvx[there, pl.ds(0, cols)] = dot(normed, w_qk1[...]).astype(BF16)
-        kvx[there, pl.ds(cols, cols)] = dot(normed, w_value1[...]).astype(BF16)
+        kvx[there, :] = dot(normed, wkv1[...]).astype(BF16)
 
     tail = length - BLOCK
-    half_rows = cols // 2
+    quarter = cols // 4
     beside = flip(me, 2)
     parity = lax.rem(lax.div(me, 2), 2)
-    early = pl.ds(pl.multiple_of(parity * half_rows, half_rows), half_rows)
-    late = pl.ds(pl.multiple_of((1 - parity) * half_rows, half_rows), half_rows)
-    w1_far = send(w_out1.at[early], w1.at[n, early], w1_sems.at[0, 0], w1_sems.at[1, 0], narrow=far)
-    w1_near = send(w_out1, w1.at[n], w1_sems.at[0, 1], w1_sems.at[1, 1], narrow=near)
-    w1_swap = send(w1.at[far, early], w1.at[far, early], w1_sems.at[0, 2], w1_sems.at[1, 2], wide=beside)
-    w1_fwd = (send(w1.at[far, early], w1.at[far, early], w1_sems.at[0, 3], w1_sems.at[1, 3], narrow=near),
-              send(w1.at[far, late], w1.at[far, late], w1_sems.at[0, 4], w1_sems.at[1, 4], narrow=near))
+    early = [pl.ds(pl.multiple_of((2 * parity + c) * quarter, quarter), quarter) for c in range(2)]
+    late = [pl.ds(pl.multiple_of((2 - 2 * parity + c) * quarter, quarter), quarter) for c in range(2)]
+    w1_far = [send(w_out1.at[early[c]], w1.at[n, early[c]], w1_sems.at[0, c], w1_sems.at[1, c], narrow=far)
+              for c in range(2)]
+    w1_near = send(w_out1, w1.at[n], w1_sems.at[0, 2], w1_sems.at[1, 2], narrow=near)
+    w1_swap = [send(w1.at[far, early[c]], w1.at[far, early[c]], w1_sems.at[0, 3 + c], w1_sems.at[1, 3 + c],
+                    wide=beside) for c in range(2)]
+    w1_fwd = [send(w1.at[far, rows], w1.at[far, rows], w1_sems.at[0, 5 + c], w1_sems.at[1, 5 + c], narrow=near)
+              for c, rows in enumerate(early + late)]
     halo = send(kvx.at[pl.ds(length, WINDOW)], kvx.at[pl.ds(0, WINDOW)], halo_sem.at[0], halo_sem.at[1],
                 wide=lax.rem(me + 1, wide_n))
+    pl.semaphore_wait(barrier, wide_n - 1 + 3)
+    for copy in w1_far:
+        copy.start()
+    for copy in loads[:3]:
+        copy.wait()
     project1(tail)
-    pl.semaphore_wait(barrier, wide_n - 1 + 3)
-    w1_far.start()
 
     @pl.when(me < wide_n - 1)
     def _():
@@ -136,36 +151,23 @@
             mixed = dot_tn(v, weights.astype(BF16)) / total
             att1[n, pl.ds(start, BLOCK), pl.ds(h * HEAD_DIM, HEAD_DIM)] = mixed.T.astype(BF16)
 
-    def share(buffer, sems, half):
-        rows = pl.ds(half * BLOCK, BLOCK)
+    def share(buffer, sems, half, size):
+        rows = pl.ds(half * size, size)
         first = send(buffer.at[n, rows], buffer.at[n, rows], sems.at[0, half, 0], sems.at[1, half, 0], narrow=far)
         second = send(buffer.at[n, rows], buffer.at[n, rows], sems.at[0, half, 1], sems.at[1, half, 1], narrow=near)
         third = send(buffer.at[far, rows], buffer.at[far, rows], sems.at[0, half, 2], sems.at[1, half, 2],
                      narrow=near)
         return first, second, third
 
-    att1_sends = [share(att1, att1_sems, half) for half in range(2)]
+    att1_sends = [share(att1, att1_sems, half, BLOCK) for half in range(2)]
     window(tail)
     att1_sends[1][0].start()
     att1_sends[1][1].start()
-    w1_far.wait_recv()
-    w1_swap.start()
-    w1_fwd[0].start()
-
-    @pl.when(me > 0)
-    def _():
-        halo.wait_recv()
-
-    window(0)
-    att1_sends[0][0].start()
-    att1_sends[0][1].start()
-
-    w1[n] = w_out1[...]
-
     most = 128
     before = (lax.broadcasted_iota(jnp.int32, (length, length), 0)
               <= lax.broadcasted_iota(jnp.int32, (length, length), 1)).astype(F32).astype(BF16)
-    for h in range(heads):
+
+    def slot_of(h):
         match = (lax.broadcasted_iota(jnp.int32, (most, length), 0) == ids[pl.ds(h, 1), :]).astype(F32)
         match16 = match.astype(BF16)
         running = dot(match16, before)
@@ -185,15 +187,37 @@
         to_slot[h] = (lax.broadcasted_iota(jnp.int32, (slots, length), 0) == target).astype(F32).astype(BF16)
         to_token[h] = (lax.broadcasted_iota(jnp.int32, (length, slots), 1) == target_col).astype(F32).astype(BF16)
 
+    loads[3].wait()
+    for c in range(2):
+        w1_far[c].wait_recv()
+        w1_swap[c].start()
+        w1_fwd[c].start()
+        if c < heads:
+            slot_of(c)
+    for h in range(2, heads):
+        slot_of(h)
+
+    @pl.when(me > 0)
+    def _():
+        halo.wait_recv()
+
+    window(0)
+    att1_sends[0][0].start()
+    att1_sends[0][1].start()
+
     att1_sends[1][0].wait_recv()
     att1_sends[1][2].start()
-    w1_swap.wait_recv()
-    w1_fwd[1].start()
+    w1_swap[0].wait_recv()
+    w1_fwd[2].start()
     att1_sends[0][0].wait_recv()
     att1_sends[0][2].start()
+    w1_swap[1].wait_recv()
+    w1_fwd[3].start()
+    for copy in loads[4:]:
+        copy.wait()
     w1_near.wait_recv()
-    w1_fwd[0].wait_recv()
-    w1_fwd[1].wait_recv()
+    for copy in w1_fwd:
+        copy.wait_recv()
 
     for half in (1, 0):
         first, second, third = att1_sends[half]
@@ -241,9 +265,7 @@
             own.wait()
 
     for h in range(heads):
-        part = pl.ds(h * HEAD_DIM, HEAD_DIM)
-        both = jnp.concatenate([w_qk2[:, part], w_value2[:, part]], axis=1)
-        packed[h] = dot(to_slot[h], dot(normed2[...], both).astype(BF16)).astype(BF16)
+        packed[h] = dot(to_slot[h], dot(normed2[...], wkv2[h]).astype(BF16)).astype(BF16)
         for level in range(3):
             @pl.loop(0, counts[level])
             def _(step):
@@ -254,7 +276,6 @@
         w2_sends.append(send(w_out2.at[:, pl.ds(pl.multiple_of(other * cols, cols), cols)], w2.at[n],
                              w2_sems.at[0, index], w2_sems.at[1, index], narrow=other))
         w2_sends[-1].start()
-    w2[n] = w_out2[:, pl.ds(pl.multiple_of(n * cols, cols), cols)]
 
     def for_level(body):
         for level in range(3):
@@ -325,23 +346,22 @@
         answers[here, :] = (mixed / total).T.astype(BF16)
 
     def own_clusters(level):
-        blocks = wide_n * pads[level] // BLOCK
-        if pads[level] == BLOCK:
-            for block in range(blocks):
-                receive(level, block)
-                attend(level, block)
-                give_back(level, block)
-        else:
-            @pl.loop(0, wide_n)
+        size = pads[level]
+        came, gone = 0, 0
+        for block in range(wide_n * size // BLOCK):
+            end = (block + 1) * BLOCK
+
+            @pl.loop(came, -(-end // size))
             def _(source):
                 receive(level, source)
 
-            for block in range(blocks):
-                attend(level, block)
-
-            @pl.loop(0, wide_n)
+            attend(level, block)
+
+            @pl.loop(gone, end // size)
             def _(source):
                 give_back(level, source)
+
+            came, gone = -(-end // size), end // size
 
     for_level(own_clusters)
 
@@ -355,28 +375,35 @@
                  back_s.at[0], back_r.at[owner], wide=there).wait_recv()
 
     each_owner(wait_back)
-    att2_sends = [share(att2, att2_sems, half) for half in range(2)]
-    for half in range(2):
-        rows = pl.ds(half * BLOCK, BLOCK)
+    pieces, piece = 4, length // 4
+    att2_sends = [share(att2, att2_sems, part, piece) for part in range(pieces)]
+    for part in range(pieces):
+        rows = pl.ds(part * piece, piece)
         for h in range(heads):
             att2[n, rows, pl.ds(h * HEAD_DIM, HEAD_DIM)] = dot(to_token[h, rows, :], ret[h]).astype(BF16)
-        att2_sends[half][0].start()
-        att2_sends[half][1].start()
+        att2_sends[part][0].start()
+        att2_sends[part][1].start()
     for copy in w2_sends:
         copy.wait_recv()
-    for half in range(2):
-        att2_sends[half][0].wait_recv()
-        att2_sends[half][2].start()
-    for half in range(2):
-        rows = pl.ds(half * BLOCK, BLOCK)
-        att2_sends[half][1].wait_recv()
-        att2_sends[half][2].wait_recv()
-        total = hidden[rows, pl.ds(pl.multiple_of(n * cols, cols), cols)].astype(F32)
+
+    def result(part):
+        rows = pl.ds(part * piece, piece)
+        att2_sends[part][1].wait_recv()
+        att2_sends[part][2].wait_recv()
+        total = hidden[rows, mine_cols].astype(F32)
         for g in range(4):
             total = total + dot(att2[g, rows, :], w2[g])
         out[rows, :] = total
 
-    for copy in (w1_far, w1_near, w1_swap, *w1_fwd, *w2_sends, *att1_sends[0], *att1_sends[1], *att2_sends[0], *att2_sends[1]):
+    for part in range(pieces):
+        att2_sends[part][0].wait_recv()
+        att2_sends[part][2].start()
+        if part > 0:
+            result(part - 1)
+    result(pieces - 1)
+
+    for copy in (*w1_far, w1_near, *w1_swap, *w1_fwd, *w2_sends,
+                 *(copy for copies in att1_sends + att2_sends for copy in copies)):
         copy.wait_send()
 
     @pl.when(me < wide_n - 1)
@@ -421,9 +448,13 @@
         return pl.pallas_call(
             functools.partial(whole_kernel, wide_n, heads, clusters, sizes, pads, slots),
             out_shape=jax.ShapeDtypeStruct((length, cols), F32),
-            in_specs=[vmem] * 8,
+            in_specs=[pl.BlockSpec(memory_space=pl.ANY)] * 8,
             out_specs=vmem,
             scratch_shapes=[
+                pltpu.VMEM((length, width), BF16),
+                pltpu.VMEM((width, 2 * cols), BF16),
+                pltpu.VMEM((heads, width, 2 * HEAD_DIM), BF16),
+                pltpu.VMEM((heads, length), jnp.int32),
                 pltpu.VMEM((WINDOW + length, 2 * cols), BF16),
                 pltpu.VMEM((groups, cols, width), BF16),
                 pltpu.VMEM((groups, length, cols), BF16),
@@ -438,9 +469,9 @@
                 pltpu.VMEM((heads, slots, HEAD_DIM), BF16),
                 pltpu.VMEM((groups, length, cols), BF16),
                 pltpu.VMEM((groups, cols, cols), BF16),
-                dma((2,)), dma((2, 5)), dma((2, 2, 3)), dma((2, 3)),
+                dma((2,)), dma((2, 9)), dma((2, 2, 3)), dma((2, 3)),
                 dma((wide_n,)), dma((wide_n,)), dma((wide_n,)), dma((wide_n,)),
-                dma((2, 2, 3)), dma,
+                dma((2, 4, 3)), dma, dma((6 + 2 * heads,)),
             ],
             compiler_params=pltpu.CompilerParams(
                 collective_id=0, has_side_effects=True, vmem_limit_bytes=56 * 1024 * 1024),

time: 57.8 us -> 55.7 us (0.964)
  Pallas kernels: 55.7 us -> 53.6 us
    pallas_call x1, Pallas kernels: 55.7 us -> 53.6 us  [shards(): pl.pallas_call(functools.partial(whole_kernel, wide_n, heads, clusters, s...]
where the time goes in v1:
time: 55.7 us; the launch traced here: 55.5 us
  Pallas kernels  53.6 us (96%)
  local copies, waits for them, and re-layouts  1.87 us (3%)
    pallas_call x1, Pallas kernels, shards(): pl.pallas_call(functools.partial(whole_kernel, wide_n, heads, clusters, s...  53.6 us
    unnamed x1, local copies, waits for them, and re-layouts  1.87 us

profile of v1, /device:TPU:0, one launch (start us, length us, event | category | flops | bytes accessed | tf_op | source)
XLA Modules:
  0.0 55.5 jit_solution(15687400777170738531)
XLA Ops:
  0.0 53.6 %shard_map.82 = f32[512,256]{1,0:T(8,128)} custom-call(bf16[512,1024]{1,0:T(8,128)(2,1)} %tokens_in.1, bf16[1024,256]{1,0:T(8,128)(2,1)} %w_qk1.1, bf16[1024,256]{1,0:T(8,128)(2,1)} %w_value1.1, bf16[256,1024]{1,0:T(8,128)(2,1)} %w_out1.1, bf16[1024,256]{1,0:T(8,128)(2,1)} %w_qk2.1, bf16[1024,256]{1,0:T(8,128)(2,1)} %w_value2.1, bf16[256,1024]{1,0:T(8,128)(2,1)} %w_out2.1, ...), custom_call_target="tpu_custom_call" | custom-call | tf_op jit(solution)/shard_map/pallas_call | solution.py:448
  53.6 1.9 %copy.10 = f32[512,256]{1,0:T(8,128)} copy(f32[512,256]{1,0:T(8,128)} %shard_map.82) | data formatting | bytes 1048576

commit v2 on v1

--- a/solution.py
+++ b/solution.py
@@ -12,6 +12,7 @@
 WINDOW = 256
 EPS = 1e-06
 BLOCK = 256
+PIECE = 128
 SCALE = math.log2(math.e) / math.sqrt(HEAD_DIM)
 LOW = -1e30
 MESH = pl.DeviceIdType.MESH
@@ -114,8 +115,8 @@
                     wide=beside) for c in range(2)]
     w1_fwd = [send(w1.at[far, rows], w1.at[far, rows], w1_sems.at[0, 5 + c], w1_sems.at[1, 5 + c], narrow=near)
               for c, rows in enumerate(early + late)]
-    halo = send(kvx.at[pl.ds(length, WINDOW)], kvx.at[pl.ds(0, WINDOW)], halo_sem.at[0], halo_sem.at[1],
-                wide=lax.rem(me + 1, wide_n))
+    halo = [send(kvx.at[pl.ds(length + start, PIECE)], kvx.at[pl.ds(start, PIECE)], halo_sem.at[0, c],
+                 halo_sem.at[1, c], wide=lax.rem(me + 1, wide_n)) for c, start in enumerate((PIECE, 0))]
     pl.semaphore_wait(barrier, wide_n - 1 + 3)
     for copy in w1_far:
         copy.start()
@@ -125,7 +126,8 @@
 
     @pl.when(me < wide_n - 1)
     def _():
-        halo.start()
+        for copy in halo:
+            copy.start()
 
     w1_near.start()
 
@@ -136,20 +138,20 @@
     project1(0)
 
     def window(start):
-        key_at = lax.broadcasted_iota(jnp.int32, (2 * BLOCK, BLOCK), 0) + (me * length + start - WINDOW)
-        query_at = lax.broadcasted_iota(jnp.int32, (2 * BLOCK, BLOCK), 1) + (me * length + start)
+        key_at = lax.broadcasted_iota(jnp.int32, (WINDOW + PIECE, PIECE), 0) + (me * length + start - WINDOW)
+        query_at = lax.broadcasted_iota(jnp.int32, (WINDOW + PIECE, PIECE), 1) + (me * length + start)
         gap = query_at - key_at
         keep = (gap > 0) & (gap < WINDOW) & (key_at >= 0) | (gap == 0) & (query_at == 0)
         for h in range(heads):
-            q = kvx[pl.ds(start + WINDOW, BLOCK), pl.ds(h * HEAD_DIM, HEAD_DIM)]
-            k = kvx[pl.ds(start, 2 * BLOCK), pl.ds(h * HEAD_DIM, HEAD_DIM)]
-            v = kvx[pl.ds(start, 2 * BLOCK), pl.ds(cols + h * HEAD_DIM, HEAD_DIM)]
+            q = kvx[pl.ds(start + WINDOW, PIECE), pl.ds(h * HEAD_DIM, HEAD_DIM)]
+            k = kvx[pl.ds(start, WINDOW + PIECE), pl.ds(h * HEAD_DIM, HEAD_DIM)]
+            v = kvx[pl.ds(start, WINDOW + PIECE), pl.ds(cols + h * HEAD_DIM, HEAD_DIM)]
             scores = jnp.where(keep, dot_nt(k, q) * SCALE, LOW)
             top = jnp.max(scores, axis=0, keepdims=True)
             weights = jnp.exp2(scores - top)
             total = jnp.sum(weights, axis=0, keepdims=True)
             mixed = dot_tn(v, weights.astype(BF16)) / total
-            att1[n, pl.ds(start, BLOCK), pl.ds(h * HEAD_DIM, HEAD_DIM)] = mixed.T.astype(BF16)
+            att1[n, pl.ds(start, PIECE), pl.ds(h * HEAD_DIM, HEAD_DIM)] = mixed.T.astype(BF16)
 
     def share(buffer, sems, half, size):
         rows = pl.ds(half * size, size)
@@ -159,10 +161,14 @@
                      narrow=near)
         return first, second, third
 
-    att1_sends = [share(att1, att1_sems, half, BLOCK) for half in range(2)]
-    window(tail)
-    att1_sends[1][0].start()
-    att1_sends[1][1].start()
+    att1_sends = [share(att1, att1_sems, part, PIECE) for part in range(4)]
+    def attend_window(part):
+        window(part * PIECE)
+        att1_sends[part][0].start()
+        att1_sends[part][1].start()
+
+    attend_window(3)
+    attend_window(2)
     most = 128
     before = (lax.broadcasted_iota(jnp.int32, (length, length), 0)
               <= lax.broadcasted_iota(jnp.int32, (length, length), 1)).astype(F32).astype(BF16)
@@ -197,20 +203,22 @@
     for h in range(2, heads):
         slot_of(h)
 
-    @pl.when(me > 0)
-    def _():
-        halo.wait_recv()
-
-    window(0)
-    att1_sends[0][0].start()
-    att1_sends[0][1].start()
-
-    att1_sends[1][0].wait_recv()
-    att1_sends[1][2].start()
+    for part in (1, 0):
+        @pl.when(me > 0)
+        def _():
+            halo[1 - part].wait_recv()
+
+        attend_window(part)
+
+    def forward(part):
+        att1_sends[part][0].wait_recv()
+        att1_sends[part][2].start()
+
+    forward(3)
+    forward(2)
     w1_swap[0].wait_recv()
     w1_fwd[2].start()
-    att1_sends[0][0].wait_recv()
-    att1_sends[0][2].start()
+    forward(1)
     w1_swap[1].wait_recv()
     w1_fwd[3].start()
     for copy in loads[4:]:
@@ -219,11 +227,11 @@
     for copy in w1_fwd:
         copy.wait_recv()
 
-    for half in (1, 0):
-        first, second, third = att1_sends[half]
-        second.wait_recv()
-        third.wait_recv()
-        rows = pl.ds(half * BLOCK, BLOCK)
+    def rest(parts):
+        for part in parts:
+            att1_sends[part][1].wait_recv()
+            att1_sends[part][2].wait_recv()
+        rows = pl.ds(parts[-1] * PIECE, len(parts) * PIECE)
         total = tokens[rows, :].astype(F32)
         for g in range(4):
             total = total + dot(att1[g, rows, :], w1[g])
@@ -231,6 +239,10 @@
         hidden[rows, :] = hidden16
         normed2[rows, :] = rms_round(hidden16)
 
+    rest((3, 2))
+    forward(0)
+    rest((1, 0))
+
     def place(level, head, step):
         rank = starts[level] + step
         owner = head * clusters + rank
@@ -264,12 +276,17 @@
             own.start()
             own.wait()
 
+    def leave(level, head):
+        @pl.loop(0, counts[level])
+        def _(step):
+            start_go(level, head, step)
+
     for h in range(heads):
         packed[h] = dot(to_slot[h], dot(normed2[...], wkv2[h]).astype(BF16)).astype(BF16)
-        for level in range(3):
-            @pl.loop(0, counts[level])
-            def _(step):
-                start_go(level, h, step)
+        leave(0, h)
+    for level in (1, 2):
+        for h in range(heads):
+            leave(level, h)
 
     w2_sends = []
     for index, other in enumerate((near, far, cross)):
@@ -408,7 +425,8 @@
 
     @pl.when(me < wide_n - 1)
     def _():
-        halo.wait_send()
+        for copy in halo:
+            copy.wait_send()
 
     def sent(level, head, step):
         there, copy, _ = go(level, head, step)
@@ -469,7 +487,7 @@
                 pltpu.VMEM((heads, slots, HEAD_DIM), BF16),
                 pltpu.VMEM((groups, length, cols), BF16),
                 pltpu.VMEM((groups, cols, cols), BF16),
-                dma((2,)), dma((2, 9)), dma((2, 2, 3)), dma((2, 3)),
+                dma((2, 2)), dma((2, 9)), dma((2, 4, 3)), dma((2, 3)),
                 dma((wide_n,)), dma((wide_n,)), dma((wide_n,)), dma((wide_n,)),
                 dma((2, 4, 3)), dma, dma((6 + 2 * heads,)),
             ],

time: 55.7 us -> 54.9 us (0.986)
  Pallas kernels: 53.6 us -> 52.9 us
    pallas_call x1, Pallas kernels: 53.6 us -> 52.9 us  [shards(): pl.pallas_call(functools.partial(whole_kernel, wide_n, heads, clusters, s...]
where the time goes in v2:
time: 54.9 us; the launch traced here: 54.8 us
  Pallas kernels  52.9 us (96%)
  local copies, waits for them, and re-layouts  1.87 us (3%)
    pallas_call x1, Pallas kernels, shards(): pl.pallas_call(functools.partial(whole_kernel, wide_n, heads, clusters, s...  52.9 us
    unnamed x1, local copies, waits for them, and re-layouts  1.87 us

profile of v2, /device:TPU:0, one launch (start us, length us, event | category | flops | bytes accessed | tf_op | source)
XLA Modules:
  0.0 54.8 jit_solution(12643087796774726226)
XLA Ops:
  0.0 52.9 %shard_map.82 = f32[512,256]{1,0:T(8,128)} custom-call(bf16[512,1024]{1,0:T(8,128)(2,1)} %tokens_in.1, bf16[1024,256]{1,0:T(8,128)(2,1)} %w_qk1.1, bf16[1024,256]{1,0:T(8,128)(2,1)} %w_value1.1, bf16[256,1024]{1,0:T(8,128)(2,1)} %w_out1.1, bf16[1024,256]{1,0:T(8,128)(2,1)} %w_qk2.1, bf16[1024,256]{1,0:T(8,128)(2,1)} %w_value2.1, bf16[256,1024]{1,0:T(8,128)(2,1)} %w_out2.1, ...), custom_call_target="tpu_custom_call" | custom-call | tf_op jit(solution)/shard_map/pallas_call | solution.py:466
  52.9 1.9 %copy.10 = f32[512,256]{1,0:T(8,128)} copy(f32[512,256]{1,0:T(8,128)} %shard_map.82) | data formatting | bytes 1048576

commit v3 on v2

--- a/solution.py
+++ b/solution.py
@@ -50,8 +50,8 @@
 
 def whole_kernel(wide_n, heads, clusters, sizes, pads, slots,
                  tokens_in, w_qk1, w_value1, w_out1, w_qk2, w_value2, w_out2, ids_in, out,
-                 tokens, wkv1, wkv2, ids, kvx, w1, att1, hidden, normed2, to_slot, to_token, packed, arrived, value_t, answers, ret, att2, w2,
-                 halo_sem, w1_sems, att1_sems, w2_sems, go_s, go_r, back_s, back_r, att2_sems, local_sem, load_sems):
+                 tokens, wkv1, wkv2, ids, kvx, w1, att1, hidden, normed2, to_slot, to_token, packed, arrived, value_t, answers, ret, before, w2,
+                 halo_sem, w1_sems, att1_sems, w2_sems, go_s, go_r, back_s, back_r, att2_sems, local_sem, load_sems, ids_sems):
     me, n = lax.axis_index("wide"), lax.axis_index("narrow")
     near, far = flip(n, 1), flip(n, 2)
     cross = flip(near, 2)
@@ -87,7 +87,7 @@
 
     mine_cols = pl.ds(pl.multiple_of(n * cols, cols), cols)
     loads = [(tokens_in, tokens), (w_qk1, wkv1.at[:, pl.ds(0, cols)]), (w_value1, wkv1.at[:, pl.ds(cols, cols)]),
-             (ids_in, ids), (w_out1, w1.at[n]), (w_out2.at[:, mine_cols], w2.at[n])]
+             (ids_in, ids.at[n]), (w_out1, w1.at[n]), (w_out2.at[:, mine_cols], w2.at[n])]
     for h in range(heads):
         part = pl.ds(h * HEAD_DIM, HEAD_DIM)
         loads.append((w_qk2.at[:, part], wkv2.at[h, :, pl.ds(0, HEAD_DIM)]))
@@ -120,6 +120,10 @@
     pl.semaphore_wait(barrier, wide_n - 1 + 3)
     for copy in w1_far:
         copy.start()
+    ids_sends = [send(ids_in, ids.at[n], ids_sems.at[0, index], ids_sems.at[1, index], narrow=other)
+                 for index, other in enumerate((near, far, cross))]
+    for copy in ids_sends:
+        copy.start()
     for copy in loads[:3]:
         copy.wait()
     project1(tail)
@@ -170,13 +174,13 @@
     attend_window(3)
     attend_window(2)
     most = 128
-    before = (lax.broadcasted_iota(jnp.int32, (length, length), 0)
+    before[...] = (lax.broadcasted_iota(jnp.int32, (length, length), 0)
               <= lax.broadcasted_iota(jnp.int32, (length, length), 1)).astype(F32).astype(BF16)
 
-    def slot_of(h):
-        match = (lax.broadcasted_iota(jnp.int32, (most, length), 0) == ids[pl.ds(h, 1), :]).astype(F32)
+    def slot_of(g, h):
+        match = (lax.broadcasted_iota(jnp.int32, (most, length), 0) == ids[g, pl.ds(h, 1), :]).astype(F32)
         match16 = match.astype(BF16)
-        running = dot(match16, before)
+        running = dot(match16, before[...])
         held = jnp.sum(match, axis=1, keepdims=True)
         held_row = dot_nt(jnp.ones((8, length), BF16), match16)[0:1, :]
         lower = (lax.broadcasted_iota(jnp.int32, (most, most), 1)
@@ -190,8 +194,12 @@
         target = jnp.sum(match * (base + running - 1.0), axis=0, keepdims=True)
         target_col = jnp.broadcast_to(target, (8, length)).T[:, 0:1].astype(jnp.int32)
         target = target.astype(jnp.int32)
+        to_token[g, h] = (lax.broadcasted_iota(jnp.int32, (length, slots), 1) == target_col).astype(F32).astype(BF16)
+        return target
+
+    def own_slots(h):
+        target = slot_of(n, h)
         to_slot[h] = (lax.broadcasted_iota(jnp.int32, (slots, length), 0) == target).astype(F32).astype(BF16)
-        to_token[h] = (lax.broadcasted_iota(jnp.int32, (length, slots), 1) == target_col).astype(F32).astype(BF16)
 
     loads[3].wait()
     for c in range(2):
@@ -199,9 +207,9 @@
         w1_swap[c].start()
         w1_fwd[c].start()
         if c < heads:
-            slot_of(c)
+            own_slots(c)
     for h in range(2, heads):
-        slot_of(h)
+        own_slots(h)
 
     for part in (1, 0):
         @pl.when(me > 0)
@@ -281,11 +289,12 @@
         def _(step):
             start_go(level, head, step)
 
-    for h in range(heads):
+    order = [lax.rem(turn + jnp.where(me < wide_n // 2, 1, 0), heads) for turn in range(heads)]
+    for h in order:
         packed[h] = dot(to_slot[h], dot(normed2[...], wkv2[h]).astype(BF16)).astype(BF16)
         leave(0, h)
     for level in (1, 2):
-        for h in range(heads):
+        for h in order:
             leave(level, h)
 
     w2_sends = []
@@ -294,6 +303,12 @@
                              w2_sems.at[0, index], w2_sems.at[1, index], narrow=other))
         w2_sends[-1].start()
 
+    for copy in ids_sends:
+        copy.wait_recv()
+    for g in (near, far, cross):
+        for h in range(heads):
+            slot_of(g, h)
+
     def for_level(body):
         for level in range(3):
             @pl.when((my_rank >= starts[level]) & (my_rank < starts[level] + counts[level]))
@@ -309,7 +324,7 @@
         size = pads[level]
         rows = pl.ds(pl.multiple_of(source * size, 16), size)
         offset = pl.multiple_of(bases[level] + (my_rank - starts[level]) * size, 16)
-        return rows, offset, send(answers.at[rows], ret.at[my_head, pl.ds(offset, size)],
+        return rows, offset, send(answers.at[rows], ret.at[n, my_head, pl.ds(offset, size)],
                                   back_s.at[source], back_r.at[mine], wide=source)
 
     def receive(level, source):
@@ -326,7 +341,7 @@
 
         @pl.when(source == me)
         def _():
-            own = pltpu.make_async_copy(answers.at[rows], ret.at[my_head, pl.ds(offset, pads[level])], local_sem)
+            own = pltpu.make_async_copy(answers.at[rows], ret.at[n, my_head, pl.ds(offset, pads[level])], local_sem)
             own.start()
             own.wait()
 
@@ -388,38 +403,51 @@
 
         @pl.when(there != me)
         def _():
-            send(answers.at[pl.ds(0, size)], ret.at[head, pl.ds(offset, size)],
+            send(answers.at[pl.ds(0, size)], ret.at[n, head, pl.ds(offset, size)],
                  back_s.at[0], back_r.at[owner], wide=there).wait_recv()
 
-    each_owner(wait_back)
-    pieces, piece = 4, length // 4
-    att2_sends = [share(att2, att2_sems, part, piece) for part in range(pieces)]
-    for part in range(pieces):
-        rows = pl.ds(part * piece, piece)
+    spans = ((0, bases[1]), (bases[1], slots - bases[1]))
+    att2_sends = []
+    for start, size in spans:
         for h in range(heads):
-            att2[n, rows, pl.ds(h * HEAD_DIM, HEAD_DIM)] = dot(to_token[h, rows, :], ret[h]).astype(BF16)
-        att2_sends[part][0].start()
-        att2_sends[part][1].start()
+            rows = pl.ds(start, size)
+            index = len(att2_sends)
+            own, other = ret.at[n, h, rows], ret.at[far, h, rows]
+            att2_sends.append((
+                send(own, own, att2_sems.at[0, index, 0], att2_sems.at[1, index, 0], narrow=far),
+                send(own, own, att2_sems.at[0, index, 1], att2_sems.at[1, index, 1], narrow=near),
+                send(other, other, att2_sems.at[0, index, 2], att2_sems.at[1, index, 2], narrow=near)))
+    for span, levels in enumerate(((0,), (1, 2))):
+        for h in range(heads):
+            for level in levels:
+                @pl.loop(0, counts[level])
+                def _(step):
+                    wait_back(level, h, step)
+            att2_sends[span * heads + h][0].start()
+            att2_sends[span * heads + h][1].start()
+
+    def result(g):
+        for half in range(length // BLOCK):
+            rows = pl.ds(half * BLOCK, BLOCK)
+            mixed = jnp.concatenate([dot(to_token[g, h, rows, :], ret[g, h]).astype(BF16) for h in range(heads)], axis=1)
+            out[rows, :] += dot(mixed, w2[g])
+
+    out[...] = hidden[:, mine_cols].astype(F32)
     for copy in w2_sends:
         copy.wait_recv()
-
-    def result(part):
-        rows = pl.ds(part * piece, piece)
-        att2_sends[part][1].wait_recv()
-        att2_sends[part][2].wait_recv()
-        total = hidden[rows, mine_cols].astype(F32)
-        for g in range(4):
-            total = total + dot(att2[g, rows, :], w2[g])
-        out[rows, :] = total
-
-    for part in range(pieces):
-        att2_sends[part][0].wait_recv()
-        att2_sends[part][2].start()
-        if part > 0:
-            result(part - 1)
-    result(pieces - 1)
-
-    for copy in (*w1_far, w1_near, *w1_swap, *w1_fwd, *w2_sends,
+    result(n)
+    for first, second, third in att2_sends:
+        first.wait_recv()
+        third.start()
+    for first, second, third in att2_sends:
+        second.wait_recv()
+    result(near)
+    result(far)
+    for first, second, third in att2_sends:
+        third.wait_recv()
+    result(cross)
+
+    for copy in (*w1_far, w1_near, *w1_swap, *w1_fwd, *w2_sends, *ids_sends,
                  *(copy for copies in att1_sends + att2_sends for copy in copies)):
         copy.wait_send()
 
@@ -445,6 +473,10 @@
                 back_copy(level, source)[2].wait_send()
 
     for_level(sent_back)
+
+
+def hand_on(answer, out):
+    out[...] = answer[...]
 
 
 def solution(mesh):
@@ -463,7 +495,7 @@
         groups = mesh.shape["narrow"]
         dma = pltpu.SemaphoreType.DMA
         vmem = pl.BlockSpec(memory_space=pltpu.VMEM)
-        return pl.pallas_call(
+        answer = pl.pallas_call(
             functools.partial(whole_kernel, wide_n, heads, clusters, sizes, pads, slots),
             out_shape=jax.ShapeDtypeStruct((length, cols), F32),
             in_specs=[pl.BlockSpec(memory_space=pl.ANY)] * 8,
@@ -472,28 +504,35 @@
                 pltpu.VMEM((length, width), BF16),
                 pltpu.VMEM((width, 2 * cols), BF16),
                 pltpu.VMEM((heads, width, 2 * HEAD_DIM), BF16),
-                pltpu.VMEM((heads, length), jnp.int32),
+                pltpu.VMEM((groups, heads, length), jnp.int32),
                 pltpu.VMEM((WINDOW + length, 2 * cols), BF16),
                 pltpu.VMEM((groups, cols, width), BF16),
                 pltpu.VMEM((groups, length, cols), BF16),
                 pltpu.VMEM((length, width), BF16),
                 pltpu.VMEM((length, width), BF16),
                 pltpu.VMEM((heads, slots, length), BF16),
-                pltpu.VMEM((heads, length, slots), BF16),
+                pltpu.VMEM((groups, heads, length, slots), BF16),
                 pltpu.VMEM((heads, slots, 2 * HEAD_DIM), BF16),
                 pltpu.VMEM((most, 2 * HEAD_DIM), BF16),
                 pltpu.VMEM((HEAD_DIM, most), BF16),
                 pltpu.VMEM((most, HEAD_DIM), BF16),
-                pltpu.VMEM((heads, slots, HEAD_DIM), BF16),
-                pltpu.VMEM((groups, length, cols), BF16),
+                pltpu.VMEM((groups, heads, slots, HEAD_DIM), BF16),
+                pltpu.VMEM((length, length), BF16),
                 pltpu.VMEM((groups, cols, cols), BF16),
                 dma((2, 2)), dma((2, 9)), dma((2, 4, 3)), dma((2, 3)),
                 dma((wide_n,)), dma((wide_n,)), dma((wide_n,)), dma((wide_n,)),
-                dma((2, 4, 3)), dma, dma((6 + 2 * heads,)),
+                dma((2, 2 * heads, 3)), dma, dma((6 + 2 * heads,)), dma((2, 3)),
             ],
             compiler_params=pltpu.CompilerParams(
                 collective_id=0, has_side_effects=True, vmem_limit_bytes=56 * 1024 * 1024),
         )(tokens, w_qk1, w_value1, w_out1, w_qk2, w_value2, w_out2, cluster_ids)
+        return pl.pallas_call(
+            hand_on,
+            grid=(2,),
+            out_shape=jax.ShapeDtypeStruct((length, cols), F32),
+            in_specs=[pl.BlockSpec((length // 2, cols), lambda i: (i, 0))],
+            out_specs=pl.BlockSpec((length // 2, cols), lambda i: (i, 0)),
+        )(answer)
 
     placed = (
         P("wide", None),

time: 54.9 us -> 52.7 us (0.960)
  the two profiles are of different devices: /device:TPU:0 before, /device:TPU:29 now
where the time goes in v3:
time: 52.7 us; the launch traced here: 52.6 us
  Pallas kernels  52.6 us (100%)
    pallas_call x1, Pallas kernels, shards(): pl.pallas_call(functools.partial(whole_kernel, wide_n, heads, clusters, s...  50.8 us
    pallas_call x1, Pallas kernels, shards(): pl.pallas_call(hand_on, grid=(2,), out_shape=jax.ShapeDtypeStruct((length...  1.77 us

profile of v3, /device:TPU:29, one launch (start us, length us, event | category | flops | bytes accessed | tf_op | source)
XLA Modules:
  0.0 52.6 jit_solution(17883388468471531674)
XLA Ops:
  0.0 50.8 %shard_map.82.answer = f32[512,256]{1,0:T(8,128)} custom-call(bf16[512,1024]{1,0:T(8,128)(2,1)} %tokens_in.1, bf16[1024,256]{1,0:T(8,128)(2,1)} %w_qk1.1, bf16[1024,256]{1,0:T(8,128)(2,1)} %w_value1.1, bf16[256,1024]{1,0:T(8,128)(2,1)} %w_out1.1, bf16[1024,256]{1,0:T(8,128)(2,1)} %w_qk2.1, bf16[1024,256]{1,0:T(8,128)(2,1)} %w_value2.1, ...), custom_call_target="tpu_custom_call" | custom-call | tf_op jit(solution)/shard_map/pallas_call | solution.py:498
  50.8 1.8 %shard_map.83 = f32[512,256]{1,0:T(8,128)} custom-call(f32[512,256]{1,0:T(8,128)} %shard_map.82.answer), custom_call_target="tpu_custom_call" | custom-call | tf_op jit(solution)/shard_map/pallas_call | solution.py:529

commit v4 on v3

--- a/solution.py
+++ b/solution.py
@@ -42,6 +42,10 @@
     return lax.dot_general(a, b, (((0,), (0,)), ((), ())), preferred_element_type=F32)
 
 
+def scaled(q):
+    return (q.astype(F32) * SCALE).astype(BF16)
+
+
 def send(src, dst, send_sem, recv_sem, **where):
     return pltpu.make_async_remote_copy(
         src_ref=src, dst_ref=dst, send_sem=send_sem, recv_sem=recv_sem,
@@ -50,7 +54,7 @@
 
 def whole_kernel(wide_n, heads, clusters, sizes, pads, slots,
                  tokens_in, w_qk1, w_value1, w_out1, w_qk2, w_value2, w_out2, ids_in, out,
-                 tokens, wkv1, wkv2, ids, kvx, w1, att1, hidden, normed2, to_slot, to_token, packed, arrived, value_t, answers, ret, before, w2,
+                 tokens, wkv1, wkv2, ids, places, kvx, w1, att1, hidden, normed2, to_slot, to_token, packed, arrived, value_t, answers, ret, before, w2,
                  halo_sem, w1_sems, att1_sems, w2_sems, go_s, go_r, back_s, back_r, att2_sems, local_sem, load_sems, ids_sems):
     me, n = lax.axis_index("wide"), lax.axis_index("narrow")
     near, far = flip(n, 1), flip(n, 2)
@@ -87,7 +91,7 @@
 
     mine_cols = pl.ds(pl.multiple_of(n * cols, cols), cols)
     loads = [(tokens_in, tokens), (w_qk1, wkv1.at[:, pl.ds(0, cols)]), (w_value1, wkv1.at[:, pl.ds(cols, cols)]),
-             (ids_in, ids.at[n]), (w_out1, w1.at[n]), (w_out2.at[:, mine_cols], w2.at[n])]
+             (ids_in, ids), (w_out1, w1.at[n]), (w_out2.at[:, mine_cols], w2.at[n])]
     for h in range(heads):
         part = pl.ds(h * HEAD_DIM, HEAD_DIM)
         loads.append((w_qk2.at[:, part], wkv2.at[h, :, pl.ds(0, HEAD_DIM)]))
@@ -120,10 +124,6 @@
     pl.semaphore_wait(barrier, wide_n - 1 + 3)
     for copy in w1_far:
         copy.start()
-    ids_sends = [send(ids_in, ids.at[n], ids_sems.at[0, index], ids_sems.at[1, index], narrow=other)
-                 for index, other in enumerate((near, far, cross))]
-    for copy in ids_sends:
-        copy.start()
     for copy in loads[:3]:
         copy.wait()
     project1(tail)
@@ -150,7 +150,7 @@
             q = kvx[pl.ds(start + WINDOW, PIECE), pl.ds(h * HEAD_DIM, HEAD_DIM)]
             k = kvx[pl.ds(start, WINDOW + PIECE), pl.ds(h * HEAD_DIM, HEAD_DIM)]
             v = kvx[pl.ds(start, WINDOW + PIECE), pl.ds(cols + h * HEAD_DIM, HEAD_DIM)]
-            scores = jnp.where(keep, dot_nt(k, q) * SCALE, LOW)
+            scores = jnp.where(keep, dot_nt(k, scaled(q)), LOW)
             top = jnp.max(scores, axis=0, keepdims=True)
             weights = jnp.exp2(scores - top)
             total = jnp.sum(weights, axis=0, keepdims=True)
@@ -177,8 +177,8 @@
     before[...] = (lax.broadcasted_iota(jnp.int32, (length, length), 0)
               <= lax.broadcasted_iota(jnp.int32, (length, length), 1)).astype(F32).astype(BF16)
 
-    def slot_of(g, h):
-        match = (lax.broadcasted_iota(jnp.int32, (most, length), 0) == ids[g, pl.ds(h, 1), :]).astype(F32)
+    def slot_of(h):
+        match = (lax.broadcasted_iota(jnp.int32, (most, length), 0) == ids[pl.ds(h, 1), :]).astype(F32)
         match16 = match.astype(BF16)
         running = dot(match16, before[...])
         held = jnp.sum(match, axis=1, keepdims=True)
@@ -192,13 +192,17 @@
             jnp.where(rank < starts[2], bases[1] + (rank - starts[1]) * pads[1],
                       bases[2] + (rank - starts[2]) * pads[2]))
         target = jnp.sum(match * (base + running - 1.0), axis=0, keepdims=True)
+        return target
+
+    def token_matrix(g, h, target):
         target_col = jnp.broadcast_to(target, (8, length)).T[:, 0:1].astype(jnp.int32)
+        to_token[g, h] = (lax.broadcasted_iota(jnp.int32, (length, slots), 1) == target_col).astype(F32).astype(BF16)
+
+    def own_slots(h):
+        target = slot_of(h)
+        token_matrix(n, h, target)
         target = target.astype(jnp.int32)
-        to_token[g, h] = (lax.broadcasted_iota(jnp.int32, (length, slots), 1) == target_col).astype(F32).astype(BF16)
-        return target
-
-    def own_slots(h):
-        target = slot_of(n, h)
+        places[n, pl.ds(h, 1), :] = target
         to_slot[h] = (lax.broadcasted_iota(jnp.int32, (slots, length), 0) == target).astype(F32).astype(BF16)
 
     loads[3].wait()
@@ -210,6 +214,10 @@
             own_slots(c)
     for h in range(2, heads):
         own_slots(h)
+    ids_sends = [send(places.at[n], places.at[n], ids_sems.at[0, index], ids_sems.at[1, index], narrow=other)
+                 for index, other in enumerate((near, far, cross))]
+    for copy in ids_sends:
+        copy.start()
 
     for part in (1, 0):
         @pl.when(me > 0)
@@ -307,7 +315,7 @@
         copy.wait_recv()
     for g in (near, far, cross):
         for h in range(heads):
-            slot_of(g, h)
+            token_matrix(g, h, places[g, pl.ds(h, 1), :].astype(F32))
 
     def for_level(body):
         for level in range(3):
@@ -349,11 +357,11 @@
         size, real = pads[level], sizes[level]
         begin = block * BLOCK
         here = pl.ds(begin, BLOCK)
-        q = arrived[here, pl.ds(0, HEAD_DIM)]
+        q = scaled(arrived[here, pl.ds(0, HEAD_DIM)])
         value_t[:, here] = arrived[here, pl.ds(HEAD_DIM, HEAD_DIM)].T
 
         def score(first, rows, diagonal):
-            scores = dot_nt(arrived[pl.ds(first, rows), pl.ds(0, HEAD_DIM)], q) * SCALE
+            scores = dot_nt(arrived[pl.ds(first, rows), pl.ds(0, HEAD_DIM)], q)
             keep = None
             key_at = lax.broadcasted_iota(jnp.int32, (rows, BLOCK), 0)
             if diagonal:
@@ -475,8 +483,14 @@
     for_level(sent_back)
 
 
-def hand_on(answer, out):
-    out[...] = answer[...]
+def hand_on(answer, out, sems):
+    size = answer.shape[0] // 8
+    copies = [pltpu.make_async_copy(answer.at[pl.ds(part * size, size)], out.at[pl.ds(part * size, size)], sems.at[part])
+              for part in range(8)]
+    for copy in copies:
+        copy.start()
+    for copy in copies:
+        copy.wait()
 
 
 def solution(mesh):
@@ -504,6 +518,7 @@
                 pltpu.VMEM((length, width), BF16),
                 pltpu.VMEM((width, 2 * cols), BF16),
                 pltpu.VMEM((heads, width, 2 * HEAD_DIM), BF16),
+                pltpu.VMEM((heads, length), jnp.int32),
                 pltpu.VMEM((groups, heads, length), jnp.int32),
                 pltpu.VMEM((WINDOW + length, 2 * cols), BF16),
                 pltpu.VMEM((groups, cols, width), BF16),
@@ -528,10 +543,10 @@
         )(tokens, w_qk1, w_value1, w_out1, w_qk2, w_value2, w_out2, cluster_ids)
         return pl.pallas_call(
             hand_on,
-            grid=(2,),
             out_shape=jax.ShapeDtypeStruct((length, cols), F32),
-            in_specs=[pl.BlockSpec((length // 2, cols), lambda i: (i, 0))],
-            out_specs=pl.BlockSpec((length // 2, cols), lambda i: (i, 0)),
+            in_specs=[pl.BlockSpec(memory_space=pl.ANY)],
+            out_specs=pl.BlockSpec(memory_space=pl.ANY),
+            scratch_shapes=[dma((8,))],
         )(answer)
 
     placed = (

time: 52.7 us -> 68.1 us (1.29)
  the two profiles are of different devices: /device:TPU:29 before, /device:TPU:0 now
where the time goes in v4:
time: 68.1 us; the launch traced here: 66.9 us
  Pallas kernels  66.7 us (98%)
    pallas_call x1, Pallas kernels, shards(): pl.pallas_call(functools.partial(whole_kernel, wide_n, heads, clusters, s...  49.6 us
    pallas_call x1, Pallas kernels, shards(): pl.pallas_call(hand_on, out_shape=jax.ShapeDtypeStruct((length, cols), F3...  17.1 us

profile of v4, /device:TPU:0, one launch (start us, length us, event | category | flops | bytes accessed | tf_op | source)
XLA Modules:
  0.0 66.9 jit_solution(6515380349669613473)
XLA Ops:
  0.0 49.6 %shard_map.82.answer = f32[512,256]{1,0:T(8,128)} custom-call(bf16[512,1024]{1,0:T(8,128)(2,1)} %tokens_in.1, bf16[1024,256]{1,0:T(8,128)(2,1)} %w_qk1.1, bf16[1024,256]{1,0:T(8,128)(2,1)} %w_value1.1, bf16[256,1024]{1,0:T(8,128)(2,1)} %w_out1.1, bf16[1024,256]{1,0:T(8,128)(2,1)} %w_qk2.1, bf16[1024,256]{1,0:T(8,128)(2,1)} %w_value2.1, ...), custom_call_target="tpu_custom_call" | custom-call | tf_op jit(solution)/shard_map/pallas_call | solution.py:512
  49.6 17.1 %shard_map.83 = f32[512,256]{1,0:T(8,128)} custom-call(f32[512,256]{1,0:T(8,128)} %shard_map.82.answer), custom_call_target="tpu_custom_call" | custom-call | tf_op jit(solution)/shard_map/pallas_call | solution.py:544

commit v5 on v4

--- a/solution.py
+++ b/solution.py
@@ -425,15 +425,31 @@
                 send(own, own, att2_sems.at[0, index, 0], att2_sems.at[1, index, 0], narrow=far),
                 send(own, own, att2_sems.at[0, index, 1], att2_sems.at[1, index, 1], narrow=near),
                 send(other, other, att2_sems.at[0, index, 2], att2_sems.at[1, index, 2], narrow=near)))
-    for span, levels in enumerate(((0,), (1, 2))):
+    def returned(span):
         for h in range(heads):
-            for level in levels:
+            for level in ((0,), (1, 2))[span]:
                 @pl.loop(0, counts[level])
                 def _(step):
                     wait_back(level, h, step)
             att2_sends[span * heads + h][0].start()
             att2_sends[span * heads + h][1].start()
 
+    def pass_on(span):
+        for first, second, third in att2_sends[span * heads:(span + 1) * heads]:
+            first.wait_recv()
+            third.start()
+
+    @pl.when(me < wide_n // 2)
+    def _():
+        returned(0)
+        returned(1)
+
+    @pl.when(me >= wide_n // 2)
+    def _():
+        returned(1)
+        pass_on(1)
+        returned(0)
+
     def result(g):
         for half in range(length // BLOCK):
             rows = pl.ds(half * BLOCK, BLOCK)
@@ -444,9 +460,12 @@
     for copy in w2_sends:
         copy.wait_recv()
     result(n)
-    for first, second, third in att2_sends:
-        first.wait_recv()
-        third.start()
+    pass_on(0)
+
+    @pl.when(me < wide_n // 2)
+    def _():
+        pass_on(1)
+
     for first, second, third in att2_sends:
         second.wait_recv()
     result(near)
@@ -483,14 +502,8 @@
     for_level(sent_back)
 
 
-def hand_on(answer, out, sems):
-    size = answer.shape[0] // 8
-    copies = [pltpu.make_async_copy(answer.at[pl.ds(part * size, size)], out.at[pl.ds(part * size, size)], sems.at[part])
-              for part in range(8)]
-    for copy in copies:
-        copy.start()
-    for copy in copies:
-        copy.wait()
+def hand_on(answer, out):
+    out[...] = answer[...]
 
 
 def solution(mesh):
@@ -544,9 +557,9 @@
         return pl.pallas_call(
             hand_on,
             out_shape=jax.ShapeDtypeStruct((length, cols), F32),
-            in_specs=[pl.BlockSpec(memory_space=pl.ANY)],
-            out_specs=pl.BlockSpec(memory_space=pl.ANY),
-            scratch_shapes=[dma((8,))],
+            grid=(2,),
+            in_specs=[pl.BlockSpec((length // 2, cols), lambda i: (i, 0))],
+            out_specs=pl.BlockSpec((length // 2, cols), lambda i: (i, 0)),
         )(answer)
 
     placed = (

time: 68.1 us -> 54.9 us (0.81)
  the two profiles are of different devices: /device:TPU:0 before, /device:TPU:25 now
where the time goes in v5:
time: 54.9 us; the launch traced here: 54.8 us
  Pallas kernels  54.8 us (100%)
    pallas_call x1, Pallas kernels, shards(): pl.pallas_call(functools.partial(whole_kernel, wide_n, heads, clusters, s...  53 us
    pallas_call x1, Pallas kernels, shards(): pl.pallas_call(hand_on, out_shape=jax.ShapeDtypeStruct((length, cols), F3...  1.77 us

profile of v5, /device:TPU:25, one launch (start us, length us, event | category | flops | bytes accessed | tf_op | source)
XLA Modules:
  0.0 54.8 jit_solution(2285105009794281190)
XLA Ops:
  0.0 53.0 %shard_map.82.answer = f32[512,256]{1,0:T(8,128)} custom-call(bf16[512,1024]{1,0:T(8,128)(2,1)} %tokens_in.1, bf16[1024,256]{1,0:T(8,128)(2,1)} %w_qk1.1, bf16[1024,256]{1,0:T(8,128)(2,1)} %w_value1.1, bf16[256,1024]{1,0:T(8,128)(2,1)} %w_out1.1, bf16[1024,256]{1,0:T(8,128)(2,1)} %w_qk2.1, bf16[1024,256]{1,0:T(8,128)(2,1)} %w_value2.1, ...), custom_call_target="tpu_custom_call" | custom-call | tf_op jit(solution)/shard_map/pallas_call | solution.py:525
  53.0 1.8 %shard_map.83 = f32[512,256]{1,0:T(8,128)} custom-call(f32[512,256]{1,0:T(8,128)} %shard_map.82.answer), custom_call_target="tpu_custom_call" | custom-call | tf_op jit(solution)/shard_map/pallas_call | solution.py:557
